TPU v7x, 512 devices: a whole 4x8x8 slice. The times are simulated.
512 devices in a mesh: gx: 8 (over x, core), gy: 8 (over z), gz: 8 (over y).
Axes of the slice: x: 4, y: 8, z: 8, core: 2. Of those that a mesh axis runs over, the one named last changes fastest.
Arguments:
- prior_basis: float32 [32, 128, 12288], P('gx', 'gy', 'gz'), may hold values from -6 to 6
- edge_weights: float32 [3, 32, 128, 128], P(None, 'gx', 'gy', 'gz'), may hold values from 0.5 to 1.5
- spectral_shift: float32 [1], replicated, may hold values from 0.5 to 4
Outputs:
- new_basis: float32 [32, 128, 16384], P('gx', 'gy', 'gz')
- projection: float32 [96, 128], replicated
- triangle: float32 [128, 128], replicated
All inputs are finite; a program needn't handle non-finite values.
Results may differ from a plain program's by a relative error of at most 0.002.
Values sent between devices are 32-bit elements; how exact they have to be, the bound alone decides.
A program may use at most 64 MiB of HBM per device.

v0:
```python
import jax
import jax.numpy as jnp
from jax import lax
from jax.sharding import PartitionSpec as P

BLOCK = 32
POWERS = 4
BASIS = 96
PRECISE = lax.Precision.HIGHEST
OPERATOR_SCALE = 11.0


def passed_along(block, axis, distance):
    devices = range(lax.axis_size(axis))
    route = [(i - distance, i) for i in devices if i - distance in devices]
    return lax.ppermute(block, axis, route)


def with_halo(block, sides, width):
    for axis, dim in sides:
        count = lax.axis_size(axis)
        forward = [(i, i + 1) for i in range(count - 1)]
        backward = [(target, source) for source, target in forward]
        low = lax.ppermute(
            lax.slice_in_dim(block, block.shape[dim] - width, None, axis=dim), axis, forward
        )
        high = lax.ppermute(lax.slice_in_dim(block, 0, width, axis=dim), axis, backward)
        block = jnp.concatenate([low, block, high], axis=dim)
    return block


def crop_margin(values, layers, columns):
    return values[
        ...,
        layers : values.shape[-3] - layers,
        layers : values.shape[-2] - layers,
        layers * columns : values.shape[-1] - layers * columns,
    ]


def stencil(padded, weight_pad, shift_value, columns):
    centre = crop_margin(padded, 1, columns)
    inner_weights = crop_margin(weight_pad, 1, columns)
    below_x = weight_pad[0, :-2, 1:-1, columns:-columns]
    below_y = weight_pad[1, 1:-1, :-2, columns:-columns]
    below_z = weight_pad[2, 1:-1, 1:-1, : -2 * columns]
    summed = inner_weights[0] * (centre - padded[2:, 1:-1, columns:-columns]) + below_x * (
        centre - padded[:-2, 1:-1, columns:-columns]
    )
    summed = (
        summed
        + inner_weights[1] * (centre - padded[1:-1, 2:, columns:-columns])
        + below_y * (centre - padded[1:-1, :-2, columns:-columns])
    )
    summed = (
        summed
        + inner_weights[2] * (centre - padded[1:-1, 1:-1, 2 * columns :])
        + below_z * (centre - padded[1:-1, 1:-1, : -2 * columns])
    )
    return (summed + shift_value * centre) / OPERATOR_SCALE - centre


def per_device(prior_basis, edge_weights, spectral_shift):
    size_x = prior_basis.shape[0]
    size_y = prior_basis.shape[1]
    size_z = prior_basis.shape[2] // BASIS
    cell_local = size_x * size_y * size_z
    cell_count = cell_local * lax.axis_size("gx") * lax.axis_size("gy") * lax.axis_size("gz")
    shift_value = spectral_shift[0]
    basis_rows = prior_basis.reshape(cell_local, BASIS)
    start_block = prior_basis.reshape(size_x, size_y, size_z, BASIS)[..., BASIS - BLOCK :]
    lower_x = passed_along(edge_weights[0, size_x - 1 :], "gx", 1)
    lower_y = passed_along(edge_weights[1, :, size_y - 1 :], "gy", 1)
    lower_z = passed_along(edge_weights[2, :, :, size_z - 1 :], "gz", 1)
    weight_pad = jnp.pad(edge_weights, ((0, 0), (1, 1), (1, 1), (1, 1)))
    weight_pad = weight_pad.at[0, 0:1, 1:-1, 1:-1].set(lower_x)
    weight_pad = weight_pad.at[1, 1:-1, 0:1, 1:-1].set(lower_y)
    weight_pad = weight_pad.at[2, 1:-1, 1:-1, 0:1].set(lower_z)
    weight_pad = jnp.repeat(weight_pad, BLOCK, axis=3)

    def apply_once(field):
        padded = with_halo(field, (("gx", 0), ("gy", 1), ("gz", 2)), 1)
        padded = padded.reshape(size_x + 2, size_y + 2, (size_z + 2) * BLOCK)
        return stencil(padded, weight_pad, shift_value, BLOCK).reshape(
            size_x, size_y, size_z, BLOCK
        )

    previous = start_block
    current = apply_once(start_block)
    powers = [current]
    for degree in range(1, POWERS):
        following = 2.0 * apply_once(current) - previous
        previous, current = (current, following)
        powers.append(following)
    krylov = jnp.stack(powers, axis=3).reshape(cell_local, BLOCK * POWERS)
    first_coef = (
        lax.psum(jnp.dot(basis_rows.T, krylov, precision=PRECISE), ("gx", "gy", "gz")) / cell_count
    )
    once = krylov - jnp.dot(basis_rows, first_coef, precision=PRECISE)
    second_coef = (
        lax.psum(jnp.dot(basis_rows.T, once, precision=PRECISE), ("gx", "gy", "gz")) / cell_count
    )
    twice = once - jnp.dot(basis_rows, second_coef, precision=PRECISE)
    gram_matrix = (
        lax.psum(jnp.dot(twice.T, twice, precision=PRECISE), ("gx", "gy", "gz")) / cell_count
    )
    lower_factor = jnp.linalg.cholesky(gram_matrix)
    solved = jax.scipy.linalg.solve_triangular(lower_factor, twice.T, lower=True)
    new_basis = solved.T.reshape(size_x, size_y, size_z * BLOCK * POWERS)
    return (new_basis, first_coef + second_coef, lower_factor.T)


def solution(mesh):
    return jax.shard_map(
        per_device,
        mesh=mesh,
        in_specs=(P("gx", "gy", "gz"), P(None, "gx", "gy", "gz"), P()),
        out_specs=(P("gx", "gy", "gz"), P(), P()),
        check_vma=False,
    )
```

profile of v0, /device:TPU:1, one launch (start us, length us, event | category | flops | bytes accessed | tf_op | source)
XLA Modules:
  0.0 644.6 jit_solution(5951552109017409170)
XLA Ops:
  8.5 4.5 collective-permute-start.3
  13.1 5.6 collective-permute-start.4
  19.6 3.7 collective-permute-start.5
  28.9 3.2 collective-permute-start.7
  33.6 4.0 collective-permute-start.2
  37.6 4.0 collective-permute-start.1
  44.4 2.5 broadcast_in_dim.5
  46.9 3.1 reshape.205
  52.9 4.1 collective-permute-start.9
  59.3 4.3 collective-permute-done.10
  63.6 5.2 collective-permute-start.11
  70.1 5.1 collective-permute-done.12
  75.4 3.2 collective-permute-start.13
  79.9 4.2 collective-permute-done.14
  85.6 4.5 collective-permute-start.15
  92.1 4.3 collective-permute-done.16
  96.4 3.4 collective-permute-start.17
  101.2 3.6 collective-permute-done.18
  104.9 4.9 collective-permute-start.19
  111.1 3.9 collective-permute-done.20
  117.0 4.8 collective-permute-start.21
  123.9 4.3 collective-permute-done.22
  128.2 4.8 collective-permute-start.23
  134.3 4.1 collective-permute-done.24
  139.2 4.3 collective-permute-start.25
  154.9 2.7 copy.16
  157.6 2.4 reshape.212
  161.2 95.3 %psum.21 = f32[96,128]{1,0:T(8,128)S(1)} all-reduce(f32[96,128]{1,0:T(8,128)S(1)} %convolution_bitcast_fusion.3), channel_id=1, replica_groups=mesh['gx'=8,'gy'=8,'gz'=8] {'gx','gy','gz'}, use_global_device_ids=true, to_apply=%region_0.1 | all-reduce | flops 12288 | bytes 98304 | tf_op jit(solution)/shard_map/psum | solution.py:97
  258.2 94.9 %psum.22 = f32[96,128]{1,0:T(8,128)S(1)} all-reduce(f32[96,128]{1,0:T(8,128)S(1)} %convolution_bitcast_fusion.2), channel_id=1, replica_groups=mesh['gx'=8,'gy'=8,'gz'=8] {'gx','gy','gz'}, use_global_device_ids=true, to_apply=%region_1.2 | all-reduce | flops 12288 | bytes 98304 | tf_op jit(solution)/shard_map/psum | solution.py:101
  355.6 254.9 %all-reduce.3.cloned.1.call-done = f32[128,128]{0,1:T(8,128)} async-done(((f32[128,128]{0,1:T(8,128)}), f32[128,128]{0,1:T(8,128)}) %all-reduce.3.cloned.1.call-update) | async-done | bytes 65552 | tf_op jit(solution)/shard_map/psum | solution.py:105
  612.3 11.7 %cholesky.16 = f32[128,128]{1,0:T(8,128)S(1)} custom-call(f32[128,128]{1,0:T(8,128)S(1)} %fusion.63), custom_call_target="Cholesky" | custom-call | tf_op jit(solution)/shard_map/jit(cholesky)/cholesky | solution.py:107
  625.4 9.8 %custom-call.7 = f32[1,128,128]{1,2,0:T(8,128)S(1)} custom-call(f32[1,128,128]{2,1,0:T(8,128)S(1)} %get-tuple-element.70), custom_call_target="InvertDiagBlocksLowerTriangular" | custom-call | tf_op jit(solution)/shard_map/jit(_solve_triangular)/triangular_solve | solution.py:108
  (132 shorter events, 53.8 us)
Async XLA Ops:
  7.2 603.3 %all-reduce.3.cloned.1.call-start = ((), (), s32[]{:S(2)}) async-start(), calls=%async_computation | async-start | bytes 131072 | tf_op jit(solution)/shard_map/psum | solution.py:105
  8.5 10.3 %collective-permute-start.3 = (f32[1,16,16,32]{3,2,1,0:T(8,128)S(1)}, f32[1,16,16,32]{3,2,1,0:T(8,128)S(1)}, u32[]{:S(2)}, u32[]{:S(2)}) collective-permute-start(f32[1,16,16,32]{3,2,1,0:T(8,128)S(1)} %get-tuple-element.65), channel_id=1, source_target_pairs={{0,64},{64,128},{128,192},{192,256},{256,320},{320,384},{384,448},... | collective-permute-start | bytes 98312 | tf_op jit(solution)/shard_map/ppermute | solution.py:24
  13.1 6.5 %collective-permute-start.4 = (f32[1,16,16,32]{3,2,1,0:T(8,128)S(1)}, f32[1,16,16,32]{3,2,1,0:T(8,128)S(1)}, u32[]{:S(2)}, u32[]{:S(2)}) collective-permute-start(f32[1,16,16,32]{3,2,1,0:T(8,128)S(1)} %get-tuple-element.66), channel_id=1, source_target_pairs={{64,0},{128,64},{192,128},{256,192},{320,256},{384,320},{448,384},... | collective-permute-start | bytes 98312 | tf_op jit(solution)/shard_map/ppermute | solution.py:27
  18.8 25.6 %copy-start.6 = (f32[1,16,16,32]{3,2,1,0:T(8,128)}, f32[1,16,16,32]{3,2,1,0:T(8,128)S(1)}, u32[]{:S(2)}) copy-start(f32[1,16,16,32]{3,2,1,0:T(8,128)S(1)} %collective-permute-done.3) | copy-start | bytes 98308
  19.6 24.8 %copy-start.7 = (f32[1,16,16,32]{3,2,1,0:T(8,128)}, f32[1,16,16,32]{3,2,1,0:T(8,128)S(1)}, u32[]{:S(2)}) copy-start(f32[1,16,16,32]{3,2,1,0:T(8,128)S(1)} %collective-permute-done.4) | copy-start | bytes 98308
  19.6 7.1 %collective-permute-start.5 = (f32[6,1,16,32]{3,2,1,0:T(8,128)S(1)}, f32[6,1,16,32]{3,2,1,0:T(8,128)S(1)}, u32[]{:S(2)}, u32[]{:S(2)}) collective-permute-start(f32[6,1,16,32]{3,2,1,0:T(8,128)S(1)} %get-tuple-element.59), channel_id=1, source_target_pairs={{0,8},{8,16},{16,24},{24,32},{32,40},{40,48},{48,56},{1,9},{9,17},... | collective-permute-start | bytes 36872 | tf_op jit(solution)/shard_map/ppermute | solution.py:24
  23.4 5.5 collective-permute-start.6
  24.7 17.8 %collective-permute-start = (f32[1,16,16]{2,1,0:T(8,128)S(1)}, f32[1,16,16]{2,1,0:T(8,128)S(1)}, u32[]{:S(2)}, u32[]{:S(2)}) collective-permute-start(f32[1,16,16]{2,1,0:T(8,128)S(1)} %slice_bitcast_fusion.6), channel_id=1, source_target_pairs={{0,64},{64,128},{128,192},{192,256},{256,320},{320,384},{384,448},... | collective-permute-start | bytes 3080 | tf_op jit(solution)/shard_map/ppermute | solution.py:16
  28.9 21.1 %collective-permute-start.7 = (f32[6,18,1,32]{3,2,1,0:T(1,128)S(1)}, f32[6,18,1,32]{3,2,1,0:T(1,128)S(1)}, u32[]{:S(2)}, u32[]{:S(2)}) collective-permute-start(f32[6,18,1,32]{3,2,1,0:T(1,128)S(1)} %get-tuple-element.51), channel_id=1, source_target_pairs={{0,1},{1,2},{2,3},{3,4},{4,5},{5,6},{6,7},{8,9},{9,10},{10,11},{11... | collective-permute-start | bytes 41480 | tf_op jit(solution)/shard_map/ppermute | solution.py:24
  32.2 18.5 %collective-permute-start.8 = (f32[6,18,1,32]{3,2,1,0:T(1,128)S(1)}, f32[6,18,1,32]{3,2,1,0:T(1,128)}, u32[]{:S(2)}, u32[]{:S(2)}) collective-permute-start(f32[6,18,1,32]{3,2,1,0:T(1,128)S(1)} %get-tuple-element.52), channel_id=1, source_target_pairs={{1,0},{2,1},{3,2},{4,3},{5,4},{6,5},{7,6},{9,8},{10,9},{11,10},{12... | collective-permute-start | bytes 41480 | tf_op jit(solution)/shard_map/ppermute | solution.py:27
  33.6 8.8 %collective-permute-start.2 = (f32[4,16,1]{1,0,2:T(4,128)S(1)}, f32[4,16,1]{1,0,2:T(4,128)S(1)}, u32[]{:S(2)}, u32[]{:S(2)}) collective-permute-start(f32[4,16,1]{1,0,2:T(4,128)S(1)} %bitcast.113), channel_id=1, source_target_pairs={{0,1},{1,2},{2,3},{3,4},{4,5},{5,6},{6,7},{8,9},{9,10},{10,11},{11... | collective-permute-start | bytes 776 | tf_op jit(solution)/shard_map/ppermute | solution.py:16
  37.6 5.7 collective-permute-start.1
  52.9 6.3 collective-permute-start.9
  57.3 6.3 collective-permute-start.10
  63.6 6.5 %collective-permute-start.11 = (f32[6,1,16,32]{3,2,1,0:T(8,128)S(1)}, f32[6,1,16,32]{3,2,1,0:T(8,128)S(1)}, u32[]{:S(2)}, u32[]{:S(2)}) collective-permute-start(f32[6,1,16,32]{3,2,1,0:T(8,128)S(1)} %get-tuple-element.57), channel_id=1, source_target_pairs={{0,8},{8,16},{16,24},{24,32},{32,40},{40,48},{48,56},{1,9},{9,17},... | collective-permute-start | bytes 36872 | tf_op jit(solution)/shard_map/ppermute | solution.py:24
  68.8 6.4 %collective-permute-start.12 = (f32[6,1,16,32]{3,2,1,0:T(8,128)S(1)}, f32[6,1,16,32]{3,2,1,0:T(8,128)S(1)}, u32[]{:S(2)}, u32[]{:S(2)}) collective-permute-start(f32[6,1,16,32]{3,2,1,0:T(8,128)S(1)} %get-tuple-element.58), channel_id=1, source_target_pairs={{8,0},{16,8},{24,16},{32,24},{40,32},{48,40},{56,48},{9,1},{17,9},... | collective-permute-start | bytes 36872 | tf_op jit(solution)/shard_map/ppermute | solution.py:27
  75.4 4.5 collective-permute-start.13
  78.6 5.5 collective-permute-start.14
  85.6 6.4 collective-permute-start.15
  90.1 6.3 collective-permute-start.16
  96.4 4.7 collective-permute-start.17
  99.8 5.0 collective-permute-start.18
  104.9 6.2 collective-permute-start.19
  109.8 5.2 collective-permute-start.20
  117.0 27.9 %copy-start.5 = (f32[4,16,1536]{2,1,0:T(8,128)S(1)}, f32[4,16,1536]{2,1,0:T(8,128)}, u32[]{:S(2)}) copy-start(f32[4,16,1536]{2,1,0:T(8,128)} %param.9) | copy-start | bytes 1179652
  117.0 6.8 %collective-permute-start.21 = (f32[1,16,16,32]{3,2,1,0:T(8,128)S(1)}, f32[1,16,16,32]{3,2,1,0:T(8,128)S(1)}, u32[]{:S(2)}, u32[]{:S(2)}) collective-permute-start(f32[1,16,16,32]{3,2,1,0:T(8,128)S(1)} %get-tuple-element.61), channel_id=1, source_target_pairs={{0,64},{64,128},{128,192},{192,256},{256,320},{320,384},{384,448},... | collective-permute-start | bytes 98312 | tf_op jit(solution)/shard_map/ppermute | solution.py:24
  121.8 23.3 %copy-start.4 = (f32[4,16,512]{2,1,0:T(8,128)S(1)}, f32[4,16,512]{2,1,0:T(8,128)}, u32[]{:S(2)}) copy-start(f32[4,16,512]{2,1,0:T(8,128)} %copy-done.3) | copy-start | bytes 393220
  121.8 6.4 collective-permute-start.22
  128.2 6.1 collective-permute-start.23
  133.0 5.4 collective-permute-start.24
  139.2 10.0 %collective-permute-start.25 = (f32[6,18,1,32]{3,2,1,0:T(1,128)}, f32[6,18,1,32]{3,2,1,0:T(1,128)}, u32[]{:S(2)}, u32[]{:S(2)}) collective-permute-start(f32[6,18,1,32]{3,2,1,0:T(1,128)} %get-tuple-element.45), channel_id=1, source_target_pairs={{0,1},{1,2},{2,3},{3,4},{4,5},{5,6},{6,7},{8,9},{9,10},{10,11},{11... | collective-permute-start | bytes 41480 | tf_op jit(solution)/shard_map/ppermute | solution.py:24
  143.4 5.7 collective-permute-start.26
  (12 other events, 85.2 us)
Sparse Core Ops, SparseCore 0:
  355.1 255.3 all-reduce.2
where the time goes:
time: 646 us; the launch traced here: 645 us
  waiting for transfers between devices  292 us (45%)
  blocking collectives  190 us (29%)
  starting transfers between devices  82.5 us (13%)
  other arithmetic  34.8 us (5%)
  local copies, waits for them, and re-layouts  24.4 us (4%)
  between operations  15.5 us (2%)
    psum x1, waiting for transfers between devices, per_device(): lax.psum(jnp.dot(twice.T, twice, precision=PRECISE), ('gx', 'gy', 'gz'))  255 us
    psum x1, blocking collectives, per_device(): lax.psum(jnp.dot(basis_rows.T, krylov, precision=PRECISE), ('gx', 'gy', '...  95.3 us
    psum x1, blocking collectives, per_device(): lax.psum(jnp.dot(basis_rows.T, once, precision=PRECISE), ('gx', 'gy', 'gz'))  94.9 us
    ppermute x12, starting transfers between devices, with_halo(): lax.ppermute(lax.slice_in_dim(block, block.shape[dim] - width, None, axis...  50.5 us
    ppermute x12, waiting for transfers between devices, with_halo(): lax.ppermute(lax.slice_in_dim(block, 0, width, axis=dim), axis, backward)  36.7 us
    ppermute x12, starting transfers between devices, with_halo(): lax.ppermute(lax.slice_in_dim(block, 0, width, axis=dim), axis, backward)  22 us
  transfers between devices with their start and end apart: 28, of which 11 were waited for; matrix products, arithmetic and copies ran while one was open for 2% of the time, Pallas kernels for 0%

commit v1 on v0

--- a/solution.py
+++ b/solution.py
@@ -102,7 +102,10 @@
     )
     twice = once - jnp.dot(basis_rows, second_coef, precision=PRECISE)
     gram_matrix = (
-        lax.psum(jnp.dot(twice.T, twice, precision=PRECISE), ("gx", "gy", "gz")) / cell_count
+        jnp.sum(
+            lax.all_gather(jnp.dot(twice.T, twice, precision=PRECISE), ("gx", "gy", "gz")), axis=0
+        )
+        / cell_count
     )
     lower_factor = jnp.linalg.cholesky(gram_matrix)
     solved = jax.scipy.linalg.solve_triangular(lower_factor, twice.T, lower=True)

time: 646 us -> 559 us (0.87)
  waiting for transfers between devices: 292 us -> 194 us
  other arithmetic: 34.8 us -> 46.2 us
    psum x1 -> x0, waiting for transfers between devices: 255 us -> none  [per_device(): lax.psum(jnp.dot(twice.T, twice, precision=PRECISE), ('gx', 'gy', 'gz'))]
    all_gather x0 -> x1, waiting for transfers between devices: none -> 157 us  [per_device(): lax.all_gather(jnp.dot(twice.T, twice, precision=PRECISE), ('gx', 'gy', '...]
    reduce_sum x0 -> x1, other arithmetic: none -> 13.1 us  [per_device(): jnp.sum(lax.all_gather(jnp.dot(twice.T, twice, precision=PRECISE), ('gx',...]
where the time goes in v1:
time: 559 us; the launch traced here: 558 us
  waiting for transfers between devices  194 us (35%)
  blocking collectives  190 us (34%)
  starting transfers between devices  82.5 us (15%)
  other arithmetic  46.2 us (8%)
  local copies, waits for them, and re-layouts  24.4 us (4%)
  between operations  15.5 us (3%)
    all_gather x1, waiting for transfers between devices, per_device(): lax.all_gather(jnp.dot(twice.T, twice, precision=PRECISE), ('gx', 'gy', '...  157 us
    psum x1, blocking collectives, per_device(): lax.psum(jnp.dot(basis_rows.T, krylov, precision=PRECISE), ('gx', 'gy', '...  95.3 us
    psum x1, blocking collectives, per_device(): lax.psum(jnp.dot(basis_rows.T, once, precision=PRECISE), ('gx', 'gy', 'gz'))  94.9 us
    ppermute x12, starting transfers between devices, with_halo(): lax.ppermute(lax.slice_in_dim(block, block.shape[dim] - width, None, axis...  50.5 us
    ppermute x12, waiting for transfers between devices, with_halo(): lax.ppermute(lax.slice_in_dim(block, 0, width, axis=dim), axis, backward)  36.7 us
    ppermute x12, starting transfers between devices, with_halo(): lax.ppermute(lax.slice_in_dim(block, 0, width, axis=dim), axis, backward)  22 us
    reduce_sum x1, other arithmetic, per_device(): jnp.sum(lax.all_gather(jnp.dot(twice.T, twice, precision=PRECISE), ('gx',...  13.1 us
    another operation x3, other arithmetic, per_device(): lower_factor = jnp.linalg.cholesky(gram_matrix)  12.4 us
  transfers between devices with their start and end apart: 28, of which 11 were waited for; matrix products, arithmetic and copies ran while one was open for 2% of the time, Pallas kernels for 0%

profile of v1, /device:TPU:1, one launch (start us, length us, event | category | flops | bytes accessed | tf_op | source)
XLA Modules:
  0.0 558.2 jit_solution(18216013535675907942)
XLA Ops:
  8.5 4.5 collective-permute-start.3
  13.1 5.6 collective-permute-start.4
  19.6 3.7 collective-permute-start.5
  28.9 3.2 collective-permute-start.7
  33.6 4.0 collective-permute-start.2
  37.6 4.0 collective-permute-start.1
  44.4 2.5 broadcast_in_dim.5
  46.9 3.1 reshape.205
  52.9 4.1 collective-permute-start.9
  59.3 4.3 collective-permute-done.10
  63.6 5.2 collective-permute-start.11
  70.1 5.1 collective-permute-done.12
  75.4 3.2 collective-permute-start.13
  79.9 4.2 collective-permute-done.14
  85.6 4.5 collective-permute-start.15
  92.1 4.3 collective-permute-done.16
  96.4 3.4 collective-permute-start.17
  101.1 3.6 collective-permute-done.18
  104.9 4.9 collective-permute-start.19
  111.1 3.9 collective-permute-done.20
  117.0 4.8 collective-permute-start.21
  123.8 4.3 collective-permute-done.22
  128.2 4.8 collective-permute-start.23
  134.3 4.1 collective-permute-done.24
  139.1 4.3 collective-permute-start.25
  154.8 2.7 copy.21
  161.2 95.3 %psum.14 = f32[96,128]{1,0:T(8,128)S(1)} all-reduce(f32[96,128]{1,0:T(8,128)S(1)} %convolution_bitcast_fusion.3), channel_id=1, replica_groups=mesh['gx'=8,'gy'=8,'gz'=8] {'gx','gy','gz'}, use_global_device_ids=true, to_apply=%region_0.1 | all-reduce | flops 12288 | bytes 98304 | tf_op jit(solution)/shard_map/psum | solution.py:97
  258.2 94.9 %psum.15 = f32[96,128]{1,0:T(8,128)S(1)} all-reduce(f32[96,128]{1,0:T(8,128)S(1)} %convolution_bitcast_fusion.2), channel_id=1, replica_groups=mesh['gx'=8,'gy'=8,'gz'=8] {'gx','gy','gz'}, use_global_device_ids=true, to_apply=%region_1.2 | all-reduce | flops 12288 | bytes 98304 | tf_op jit(solution)/shard_map/psum | solution.py:101
  355.6 157.0 %all-gather.3.cloned.1.call-done = f32[65536,128]{1,0:T(8,128)} async-done(((f32[128,128]{1,0:T(8,128)}), f32[65536,128]{1,0:T(8,128)}) %all-gather.3.cloned.1.call-update) | async-done | bytes 33554448 | tf_op jit(solution)/shard_map/all_gather | solution.py:106
  512.6 13.1 %reduce_sum.11 = f32[128,128]{1,0:T(8,128)S(1)} reduce(f32[512,128,128]{2,1,0:T(8,128)} %bitcast.110, f32[]{:T(128)} %constant.147.clone.1), dimensions={0}, to_apply=%region_2.3 | reduce | flops 8372224 | bytes 33619972 | tf_op jit(solution)/shard_map/reduce_sum | solution.py:105
  525.8 11.7 %cholesky.16 = f32[128,128]{1,0:T(8,128)S(1)} custom-call(f32[128,128]{1,0:T(8,128)S(1)} %fusion.63), custom_call_target="Cholesky" | custom-call | tf_op jit(solution)/shard_map/jit(cholesky)/cholesky | solution.py:110
  539.6 9.8 %custom-call.7 = f32[1,128,128]{1,2,0:T(8,128)S(1)} custom-call(f32[1,128,128]{2,1,0:T(8,128)S(1)} %get-tuple-element.73), custom_call_target="InvertDiagBlocksLowerTriangular" | custom-call | tf_op jit(solution)/shard_map/jit(_solve_triangular)/triangular_solve | solution.py:111
  (132 shorter events, 54.6 us)
Async XLA Ops:
  7.2 505.5 %all-gather.3.cloned.1.call-start = ((), (), s32[]{:S(2)}) async-start(), calls=%async_computation | async-start | bytes 33619968 | tf_op jit(solution)/shard_map/all_gather | solution.py:106
  8.5 10.3 %collective-permute-start.3 = (f32[1,16,16,32]{3,2,1,0:T(8,128)S(1)}, f32[1,16,16,32]{3,2,1,0:T(8,128)S(1)}, u32[]{:S(2)}, u32[]{:S(2)}) collective-permute-start(f32[1,16,16,32]{3,2,1,0:T(8,128)S(1)} %get-tuple-element.68), channel_id=1, source_target_pairs={{0,64},{64,128},{128,192},{192,256},{256,320},{320,384},{384,448},... | collective-permute-start | bytes 98312 | tf_op jit(solution)/shard_map/ppermute | solution.py:24
  13.1 6.5 %collective-permute-start.4 = (f32[1,16,16,32]{3,2,1,0:T(8,128)S(1)}, f32[1,16,16,32]{3,2,1,0:T(8,128)S(1)}, u32[]{:S(2)}, u32[]{:S(2)}) collective-permute-start(f32[1,16,16,32]{3,2,1,0:T(8,128)S(1)} %get-tuple-element.69), channel_id=1, source_target_pairs={{64,0},{128,64},{192,128},{256,192},{320,256},{384,320},{448,384},... | collective-permute-start | bytes 98312 | tf_op jit(solution)/shard_map/ppermute | solution.py:27
  18.8 25.6 %copy-start.6 = (f32[1,16,16,32]{3,2,1,0:T(8,128)}, f32[1,16,16,32]{3,2,1,0:T(8,128)S(1)}, u32[]{:S(2)}) copy-start(f32[1,16,16,32]{3,2,1,0:T(8,128)S(1)} %collective-permute-done.3) | copy-start | bytes 98308
  19.6 24.8 %copy-start.7 = (f32[1,16,16,32]{3,2,1,0:T(8,128)}, f32[1,16,16,32]{3,2,1,0:T(8,128)S(1)}, u32[]{:S(2)}) copy-start(f32[1,16,16,32]{3,2,1,0:T(8,128)S(1)} %collective-permute-done.4) | copy-start | bytes 98308
  19.6 7.1 %collective-permute-start.5 = (f32[6,1,16,32]{3,2,1,0:T(8,128)S(1)}, f32[6,1,16,32]{3,2,1,0:T(8,128)S(1)}, u32[]{:S(2)}, u32[]{:S(2)}) collective-permute-start(f32[6,1,16,32]{3,2,1,0:T(8,128)S(1)} %get-tuple-element.62), channel_id=1, source_target_pairs={{0,8},{8,16},{16,24},{24,32},{32,40},{40,48},{48,56},{1,9},{9,17},... | collective-permute-start | bytes 36872 | tf_op jit(solution)/shard_map/ppermute | solution.py:24
  23.4 5.5 collective-permute-start.6
  24.7 17.8 %collective-permute-start = (f32[1,16,16]{2,1,0:T(8,128)S(1)}, f32[1,16,16]{2,1,0:T(8,128)S(1)}, u32[]{:S(2)}, u32[]{:S(2)}) collective-permute-start(f32[1,16,16]{2,1,0:T(8,128)S(1)} %slice_bitcast_fusion.6), channel_id=1, source_target_pairs={{0,64},{64,128},{128,192},{192,256},{256,320},{320,384},{384,448},... | collective-permute-start | bytes 3080 | tf_op jit(solution)/shard_map/ppermute | solution.py:16
  28.9 21.1 %collective-permute-start.7 = (f32[6,18,1,32]{3,2,1,0:T(1,128)S(1)}, f32[6,18,1,32]{3,2,1,0:T(1,128)S(1)}, u32[]{:S(2)}, u32[]{:S(2)}) collective-permute-start(f32[6,18,1,32]{3,2,1,0:T(1,128)S(1)} %get-tuple-element.54), channel_id=1, source_target_pairs={{0,1},{1,2},{2,3},{3,4},{4,5},{5,6},{6,7},{8,9},{9,10},{10,11},{11... | collective-permute-start | bytes 41480 | tf_op jit(solution)/shard_map/ppermute | solution.py:24
  32.2 18.5 %collective-permute-start.8 = (f32[6,18,1,32]{3,2,1,0:T(1,128)S(1)}, f32[6,18,1,32]{3,2,1,0:T(1,128)}, u32[]{:S(2)}, u32[]{:S(2)}) collective-permute-start(f32[6,18,1,32]{3,2,1,0:T(1,128)S(1)} %get-tuple-element.55), channel_id=1, source_target_pairs={{1,0},{2,1},{3,2},{4,3},{5,4},{6,5},{7,6},{9,8},{10,9},{11,10},{12... | collective-permute-start | bytes 41480 | tf_op jit(solution)/shard_map/ppermute | solution.py:27
  33.6 8.8 %collective-permute-start.2 = (f32[4,16,1]{1,0,2:T(4,128)S(1)}, f32[4,16,1]{1,0,2:T(4,128)S(1)}, u32[]{:S(2)}, u32[]{:S(2)}) collective-permute-start(f32[4,16,1]{1,0,2:T(4,128)S(1)} %bitcast.115), channel_id=1, source_target_pairs={{0,1},{1,2},{2,3},{3,4},{4,5},{5,6},{6,7},{8,9},{9,10},{10,11},{11... | collective-permute-start | bytes 776 | tf_op jit(solution)/shard_map/ppermute | solution.py:16
  37.6 5.7 %collective-permute-start.1 = (f32[4,1,16]{2,0,1:T(4,128)S(1)}, f32[4,1,16]{2,0,1:T(4,128)S(1)}, u32[]{:S(2)}, u32[]{:S(2)}) collective-permute-start(f32[4,1,16]{2,0,1:T(4,128)S(1)} %bitcast.116), channel_id=1, source_target_pairs={{0,8},{8,16},{16,24},{24,32},{32,40},{40,48},{48,56},{1,9},{9,17},... | collective-permute-start | bytes 776 | tf_op jit(solution)/shard_map/ppermute | solution.py:16
  52.9 6.3 %collective-permute-start.9 = (f32[1,16,16,32]{3,2,1,0:T(8,128)S(1)}, f32[1,16,16,32]{3,2,1,0:T(8,128)S(1)}, u32[]{:S(2)}, u32[]{:S(2)}) collective-permute-start(f32[1,16,16,32]{3,2,1,0:T(8,128)S(1)} %slice.363), channel_id=1, source_target_pairs={{0,64},{64,128},{128,192},{192,256},{256,320},{320,384},{384,448},... | collective-permute-start | bytes 98312 | tf_op jit(solution)/shard_map/ppermute | solution.py:24
  57.3 6.3 %collective-permute-start.10 = (f32[1,16,16,32]{3,2,1,0:T(8,128)S(1)}, f32[1,16,16,32]{3,2,1,0:T(8,128)S(1)}, u32[]{:S(2)}, u32[]{:S(2)}) collective-permute-start(f32[1,16,16,32]{3,2,1,0:T(8,128)S(1)} %slice.365), channel_id=1, source_target_pairs={{64,0},{128,64},{192,128},{256,192},{320,256},{384,320},{448,384},... | collective-permute-start | bytes 98312 | tf_op jit(solution)/shard_map/ppermute | solution.py:27
  63.6 6.5 %collective-permute-start.11 = (f32[6,1,16,32]{3,2,1,0:T(8,128)S(1)}, f32[6,1,16,32]{3,2,1,0:T(8,128)S(1)}, u32[]{:S(2)}, u32[]{:S(2)}) collective-permute-start(f32[6,1,16,32]{3,2,1,0:T(8,128)S(1)} %get-tuple-element.60), channel_id=1, source_target_pairs={{0,8},{8,16},{16,24},{24,32},{32,40},{40,48},{48,56},{1,9},{9,17},... | collective-permute-start | bytes 36872 | tf_op jit(solution)/shard_map/ppermute | solution.py:24
  68.8 6.4 %collective-permute-start.12 = (f32[6,1,16,32]{3,2,1,0:T(8,128)S(1)}, f32[6,1,16,32]{3,2,1,0:T(8,128)S(1)}, u32[]{:S(2)}, u32[]{:S(2)}) collective-permute-start(f32[6,1,16,32]{3,2,1,0:T(8,128)S(1)} %get-tuple-element.61), channel_id=1, source_target_pairs={{8,0},{16,8},{24,16},{32,24},{40,32},{48,40},{56,48},{9,1},{17,9},... | collective-permute-start | bytes 36872 | tf_op jit(solution)/shard_map/ppermute | solution.py:27
  75.4 4.5 collective-permute-start.13
  78.6 5.5 collective-permute-start.14
  85.6 6.4 %collective-permute-start.15 = (f32[1,16,16,32]{3,2,1,0:T(8,128)S(1)}, f32[1,16,16,32]{3,2,1,0:T(8,128)S(1)}, u32[]{:S(2)}, u32[]{:S(2)}) collective-permute-start(f32[1,16,16,32]{3,2,1,0:T(8,128)S(1)} %get-tuple-element.66), channel_id=1, source_target_pairs={{0,64},{64,128},{128,192},{192,256},{256,320},{320,384},{384,448},... | collective-permute-start | bytes 98312 | tf_op jit(solution)/shard_map/ppermute | solution.py:24
  90.1 6.3 %collective-permute-start.16 = (f32[1,16,16,32]{3,2,1,0:T(8,128)S(1)}, f32[1,16,16,32]{3,2,1,0:T(8,128)S(1)}, u32[]{:S(2)}, u32[]{:S(2)}) collective-permute-start(f32[1,16,16,32]{3,2,1,0:T(8,128)S(1)} %get-tuple-element.67), channel_id=1, source_target_pairs={{64,0},{128,64},{192,128},{256,192},{320,256},{384,320},{448,384},... | collective-permute-start | bytes 98312 | tf_op jit(solution)/shard_map/ppermute | solution.py:27
  96.4 4.7 collective-permute-start.17
  99.8 5.0 collective-permute-start.18
  104.9 6.2 %collective-permute-start.19 = (f32[6,18,1,32]{3,2,1,0:T(1,128)S(1)}, f32[6,18,1,32]{3,2,1,0:T(1,128)S(1)}, u32[]{:S(2)}, u32[]{:S(2)}) collective-permute-start(f32[6,18,1,32]{3,2,1,0:T(1,128)S(1)} %get-tuple-element.50), channel_id=1, source_target_pairs={{0,1},{1,2},{2,3},{3,4},{4,5},{5,6},{6,7},{8,9},{9,10},{10,11},{11... | collective-permute-start | bytes 41480 | tf_op jit(solution)/shard_map/ppermute | solution.py:24
  109.8 5.2 collective-permute-start.20
  117.0 27.9 %copy-start.5 = (f32[4,16,1536]{2,1,0:T(8,128)S(1)}, f32[4,16,1536]{2,1,0:T(8,128)}, u32[]{:S(2)}) copy-start(f32[4,16,1536]{2,1,0:T(8,128)} %param.9) | copy-start | bytes 1179652
  117.0 6.8 %collective-permute-start.21 = (f32[1,16,16,32]{3,2,1,0:T(8,128)S(1)}, f32[1,16,16,32]{3,2,1,0:T(8,128)S(1)}, u32[]{:S(2)}, u32[]{:S(2)}) collective-permute-start(f32[1,16,16,32]{3,2,1,0:T(8,128)S(1)} %get-tuple-element.64), channel_id=1, source_target_pairs={{0,64},{64,128},{128,192},{192,256},{256,320},{320,384},{384,448},... | collective-permute-start | bytes 98312 | tf_op jit(solution)/shard_map/ppermute | solution.py:24
  121.8 23.3 %copy-start.4 = (f32[4,16,512]{2,1,0:T(8,128)S(1)}, f32[4,16,512]{2,1,0:T(8,128)}, u32[]{:S(2)}) copy-start(f32[4,16,512]{2,1,0:T(8,128)} %copy-done.3) | copy-start | bytes 393220
  121.8 6.4 %collective-permute-start.22 = (f32[1,16,16,32]{3,2,1,0:T(8,128)S(1)}, f32[1,16,16,32]{3,2,1,0:T(8,128)S(1)}, u32[]{:S(2)}, u32[]{:S(2)}) collective-permute-start(f32[1,16,16,32]{3,2,1,0:T(8,128)S(1)} %get-tuple-element.65), channel_id=1, source_target_pairs={{64,0},{128,64},{192,128},{256,192},{320,256},{384,320},{448,384},... | collective-permute-start | bytes 98312 | tf_op jit(solution)/shard_map/ppermute | solution.py:27
  128.2 6.1 %collective-permute-start.23 = (f32[6,1,16,32]{3,2,1,0:T(8,128)S(1)}, f32[6,1,16,32]{3,2,1,0:T(8,128)S(1)}, u32[]{:S(2)}, u32[]{:S(2)}) collective-permute-start(f32[6,1,16,32]{3,2,1,0:T(8,128)S(1)} %get-tuple-element.56), channel_id=1, source_target_pairs={{0,8},{8,16},{16,24},{24,32},{32,40},{40,48},{48,56},{1,9},{9,17},... | collective-permute-start | bytes 36872 | tf_op jit(solution)/shard_map/ppermute | solution.py:24
  133.0 5.4 collective-permute-start.24
  139.1 10.0 %collective-permute-start.25 = (f32[6,18,1,32]{3,2,1,0:T(1,128)}, f32[6,18,1,32]{3,2,1,0:T(1,128)}, u32[]{:S(2)}, u32[]{:S(2)}) collective-permute-start(f32[6,18,1,32]{3,2,1,0:T(1,128)} %get-tuple-element.48), channel_id=1, source_target_pairs={{0,1},{1,2},{2,3},{3,4},{4,5},{5,6},{6,7},{8,9},{9,10},{10,11},{11... | collective-permute-start | bytes 41480 | tf_op jit(solution)/shard_map/ppermute | solution.py:24
  143.4 5.7 %collective-permute-start.26 = (f32[6,18,1,32]{3,2,1,0:T(1,128)}, f32[6,18,1,32]{3,2,1,0:T(1,128)}, u32[]{:S(2)}, u32[]{:S(2)}) collective-permute-start(f32[6,18,1,32]{3,2,1,0:T(1,128)} %get-tuple-element.49), channel_id=1, source_target_pairs={{1,0},{2,1},{3,2},{4,3},{5,4},{6,5},{7,6},{9,8},{10,9},{11,10},{12... | collective-permute-start | bytes 41480 | tf_op jit(solution)/shard_map/ppermute | solution.py:27
  (12 other events, 89.2 us)
Sparse Core Ops, SparseCore 0:
  355.1 157.4 all-gather.2
